TPU v7x, 256 devices: a whole 4x4x8 slice. The times are simulated.
256 devices in a mesh: node: 64 (over y, z_hi, x, core), local: 4 (over z_lo).
Axes of the slice: x: 4, y: 4, z: 8 (z_hi: 2, z_lo: 4; z = z_hi * 4 + z_lo), core: 2. Of those that a mesh axis runs over, the one named last changes fastest.
Arguments:
- tokens: bfloat16 [65536, 4096], P(('node', 'local')), may hold values from -24 to 24
- queries: bfloat16 [65536, 4096], P(('node', 'local')), may hold values from -240 to 240
- values: bfloat16 [65536, 512], P(('node', 'local')), may hold values from -6 to 6
- upstream: bfloat16 [65536, 4096], P(('node', 'local')), may hold values from -6 to 6
- key_weight: bfloat16 [4096, 512], P(('node', 'local')), may hold values from -0.09375 to 0.09375
- positions: int32 [65536], P(('node', 'local')), may hold values from 0 to 255, as said below
Outputs:
- grad_tokens: bfloat16 [65536, 4096], P(('node', 'local'))
- grad_weight: float32 [4096, 512], P(('node', 'local'))
Inputs may be any that keep to these rules, and one draw needn't show every extreme that they name: positions[i] counts the earlier tokens of token i's document; every block of 256 rows starts a document, and no document crosses such a block.
All inputs are finite; a program needn't handle non-finite values.
Results may differ from a plain program's by a relative error of at most 0.033.
Values may be sent and summed in bfloat16 or wider, within the bound.
A program may use at most 128 MiB of HBM per device.

v0:
```python
import jax
import jax.numpy as jnp
from jax import lax
from jax.sharding import Mesh
from jax.sharding import PartitionSpec as P

HEAD_SIZE = 128
NODE = ("node_0", "node_1", "node_2", "node_3")
NODE_LOCAL = ("node_0", "node_1", "node_2", "node_3", "local")


def piece_ends(length, count):
    unit = 8 if length >= 8 * count else 1
    return [length // unit * k // count * unit for k in range(1, count)]


def stacked_from(shard, axes, sequence):
    tiles = shard
    for k in sequence:
        tiles = lax.all_gather(tiles, axes[k])
    done = sequence[::-1]
    back = [done.index(k) for k in range(len(axes))]
    tiles = tiles.transpose(*back, *range(len(axes), tiles.ndim))
    return tiles.reshape(-1, *shard.shape)


def in_order(tiles, dim):
    tiles = jnp.moveaxis(tiles, 0, dim)
    dims = tiles.shape
    return tiles.reshape(*dims[:dim], dims[dim] * dims[dim + 1], *dims[dim + 2 :])


def gather_at_once(shard, axes, dim):
    numbers = list(range(len(axes)))[::-1]
    widest = shard.shape.index(max(shard.shape[:-1] or shard.shape))
    edges = [0, *piece_ends(shard.shape[widest], len(axes)), shard.shape[widest]]
    outs = []
    for k, (start, end) in enumerate(zip(edges, edges[1:])):
        if end > start:
            section = lax.slice_in_dim(shard, start, end, axis=widest)
            outs.append(stacked_from(section, axes, numbers[k:] + numbers[:k]))
    return in_order(jnp.concatenate(outs, axis=widest + 1), dim)


def cut_along(shard, dim, size):
    dims = shard.shape
    tiles = shard.reshape(*dims[:dim], size, dims[dim] // size, *dims[dim + 1 :])
    return jnp.moveaxis(tiles, dim, 0)


def sent_and_summed(shard, axis, dim):
    tiles = cut_along(shard, dim, lax.axis_size(axis))
    arrived = lax.all_to_all(tiles, axis, split_axis=0, concat_axis=0, tiled=True)
    return arrived.sum(axis=0)


def angle_tables(positions, head_width):
    half = head_width // 2
    freq = jnp.exp(
        -(jnp.arange(half, dtype=jnp.float32) * 2.0 / head_width) * jnp.log(jnp.float32(1000000.0))
    )
    angle = positions.astype(jnp.float32)[:, None] * freq[None, :]
    return (jnp.cos(angle)[:, None, :], jnp.sin(angle)[:, None, :])


def rotate(raw_keys, cosine, sine_part, head_width, sign):
    item_count, width = raw_keys.shape
    shaped = raw_keys.reshape(item_count, width // head_width, head_width)
    half = head_width // 2
    first, second = (shaped[..., :half], shaped[..., half:])
    joined = jnp.concatenate(
        [first * cosine - sign * second * sine_part, second * cosine + sign * first * sine_part],
        axis=-1,
    )
    return joined.reshape(item_count, width)


def attend_back(queries, keys, values, upstream, positions, head_width):
    item_count, width = keys.shape
    key_value_count = width // head_width
    group_size = queries.shape[1] // width
    scale = head_width ** (-0.5)
    qmat = queries.reshape(item_count, key_value_count, group_size, head_width)
    kmat = keys.reshape(item_count, key_value_count, head_width)
    value_matrix = values.reshape(item_count, key_value_count, head_width)
    upper_matrix = upstream.reshape(item_count, key_value_count, group_size, head_width)
    scores = jnp.einsum("yxru,oxu->xryo", qmat, kmat, preferred_element_type=jnp.float32) * scale
    place = jnp.arange(item_count, dtype=jnp.int32)
    allowed = (place[None, :] <= place[:, None]) & (place[None, :] >= (place - positions)[:, None])
    scores = jnp.where(allowed, scores, jnp.float32(-1e30))
    top = jnp.max(scores, axis=-1, keepdims=True)
    expo = jnp.exp(scores - top)
    probs = expo / jnp.sum(expo, axis=-1, keepdims=True)
    slope_values = jnp.einsum(
        "yxru,oxu->xryo", upper_matrix, value_matrix, preferred_element_type=jnp.float32
    )
    inner = jnp.sum(probs * slope_values, axis=-1, keepdims=True)
    dscores = (probs * (slope_values - inner) * scale).astype(jnp.bfloat16)
    grad_rot = jnp.einsum("kgts,tkgd->skd", dscores, qmat, preferred_element_type=jnp.float32)
    return grad_rot.reshape(item_count, width)


def per_device(tokens, queries, values, upstream, key_weight, positions):
    node_count = lax.axis_size(NODE)
    local_count = lax.axis_size("local")
    local_index = lax.axis_index("local")
    shard_rows = key_weight.shape[0]
    key_width = key_weight.shape[1]
    item_count = tokens.shape[0]
    model_width = tokens.shape[1]
    head_width = HEAD_SIZE
    whole_weight = gather_at_once(key_weight, NODE_LOCAL, 0)
    raw_keys = jnp.dot(tokens, whole_weight, preferred_element_type=jnp.float32)
    grouped = whole_weight.reshape(node_count, local_count, shard_rows, key_width)
    quarter = lax.dynamic_index_in_dim(grouped, local_index, 1, keepdims=False)
    quarter = quarter.reshape(node_count * shard_rows, key_width)
    cosine, sine_part = angle_tables(positions, head_width)
    keys = rotate(raw_keys, cosine, sine_part, head_width, 1.0).astype(jnp.bfloat16)
    grad_rot = attend_back(queries, keys, values, upstream, positions, head_width)
    grad_keys = rotate(grad_rot, cosine, sine_part, head_width, -1.0).astype(jnp.bfloat16)
    mixed = lax.dot_general(
        grad_keys,
        lax.all_gather(quarter, "local", axis=0, tiled=True),
        (((1,), (1,)), ((), ())),
        preferred_element_type=jnp.float32,
    ).astype(jnp.bfloat16)
    grad_tokens = mixed.reshape(item_count, local_count, node_count, shard_rows)
    grad_tokens = jnp.transpose(grad_tokens, (0, 2, 1, 3)).reshape(item_count, model_width)
    sectioned = lax.psum_scatter(
        lax.dot_general(
            tokens, grad_keys, (((0,), (0,)), ((), ())), preferred_element_type=jnp.float32
        ),
        NODE,
        scatter_dimension=0,
        tiled=True,
    )
    grad_weight = sent_and_summed(sectioned, "local", 0)
    return (grad_tokens, grad_weight)


def solution(mesh):
    torus = Mesh(
        mesh.devices.reshape(4, 2, 4, 2, mesh.shape["local"]),
        ("node_0", "node_1", "node_2", "node_3", "local"),
    )
    placed = (
        P(NODE_LOCAL, None),
        P(NODE_LOCAL, None),
        P(NODE_LOCAL, None),
        P(NODE_LOCAL, None),
        P(NODE_LOCAL, None),
        P(NODE_LOCAL),
    )
    return jax.shard_map(
        per_device,
        mesh=torus,
        in_specs=placed,
        out_specs=(P(NODE_LOCAL, None), P(NODE_LOCAL, None)),
        check_vma=False,
    )
```

profile of v0, /device:TPU:1, one launch (start us, length us, event | category | flops | bytes accessed | tf_op | source)
XLA Modules:
  0.0 926.5 jit_solution(6340969713008578064)
XLA Ops:
  8.1 10.4 %all-gather.29 = bf16[4,4,512]{2,1,0:T(4,128)(2,1)S(1)} all-gather(bf16[1,4,512]{2,1,0:T(4,128)(2,1)S(1)} %slice_bitcast_fusion), channel_id=22, replica_groups=mesh['node_0'=4,'node_1'=2,'node_2'=4,'node_3'=2,'local'=4] {'node_0'}, dimensions={0}, use_global_device_ids=true | all-gather | bytes 20480 | tf_op jit(solution)/shard_map/all_gather | solution.py:20
  18.4 11.4 %all-gather.21 = bf16[16,4,512]{2,1,0:T(4,128)(2,1)S(1)} all-gather(bf16[4,4,512]{2,1,0:T(4,128)(2,1)S(1)} %all-gather.29), channel_id=23, replica_groups=mesh['node_0'=4,'node_1'=2,'node_2'=4,'node_3'=2,'local'=4] {'local'}, dimensions={0}, use_global_device_ids=true | all-gather | bytes 81920 | tf_op jit(solution)/shard_map/all_gather | solution.py:20
  29.9 8.1 all-gather.22
  38.0 10.9 %all-gather.23 = bf16[8,4,4,4,512]{4,3,2,1,0:T(4,128)(2,1)} all-gather(bf16[2,4,4,4,512]{4,3,2,1,0:T(4,128)(2,1)S(1)} %bitcast.150), channel_id=25, replica_groups=mesh['node_0'=4,'node_1'=2,'node_2'=4,'node_3'=2,'local'=4] {'node_2'}, dimensions={0}, use_global_device_ids=true | all-gather | bytes 655360 | tf_op jit(solution)/shard_map/all_gather | solution.py:20
  54.3 9.0 all-gather.6
  63.3 7.9 all-gather.7
  71.3 10.6 %all-gather.8 = bf16[8,4,2,3,512]{4,1,3,2,0:T(4,128)(2,1)S(1)} all-gather(bf16[2,4,2,3,512]{4,1,3,2,0:T(4,128)(2,1)S(1)} %copy.136), channel_id=10, replica_groups=mesh['node_0'=4,'node_1'=2,'node_2'=4,'node_3'=2,'local'=4] {'node_0'}, dimensions={0}, use_global_device_ids=true | all-gather | bytes 245760 | tf_op jit(solution)/shard_map/all_gather | solution.py:20
  81.9 21.4 %all-gather.9 = bf16[16,2,4,2,3,512]{5,2,4,3,1,0:T(4,128)(2,1)S(1)} all-gather(bf16[4,2,4,2,3,512]{5,2,4,3,1,0:T(4,128)(2,1)S(1)} %bitcast.149), channel_id=11, replica_groups=mesh['node_0'=4,'node_1'=2,'node_2'=4,'node_3'=2,'local'=4] {'local'}, dimensions={0}, use_global_device_ids=true | all-gather | bytes 983040 | tf_op jit(solution)/shard_map/all_gather | solution.py:20
  104.6 9.6 %all-gather.27 = bf16[4,3,512]{2,1,0:T(4,128)(2,1)S(1)} all-gather(bf16[1,3,512]{2,1,0:T(4,128)(2,1)S(1)} %get-tuple-element.19), channel_id=12, replica_groups=mesh['node_0'=4,'node_1'=2,'node_2'=4,'node_3'=2,'local'=4] {'node_2'}, dimensions={0}, use_global_device_ids=true | all-gather | bytes 15360 | tf_op jit(solution)/shard_map/all_gather | solution.py:20
  114.2 7.2 all-gather.11
  121.4 9.3 %all-gather.12 = bf16[8,4,3,512]{3,1,2,0:T(4,128)(2,1)S(1)} all-gather(bf16[2,4,3,512]{3,1,2,0:T(4,128)(2,1)S(1)} %copy.139), channel_id=14, replica_groups=mesh['node_0'=4,'node_1'=2,'node_2'=4,'node_3'=2,'local'=4] {'node_0'}, dimensions={0}, use_global_device_ids=true | all-gather | bytes 122880 | tf_op jit(solution)/shard_map/all_gather | solution.py:20
  130.7 11.4 %all-gather.13 = bf16[16,2,4,3,512]{4,2,3,1,0:T(4,128)(2,1)S(1)} all-gather(bf16[4,2,4,3,512]{4,2,3,1,0:T(4,128)(2,1)S(1)} %bitcast.154), channel_id=15, replica_groups=mesh['node_0'=4,'node_1'=2,'node_2'=4,'node_3'=2,'local'=4] {'local'}, dimensions={0}, use_global_device_ids=true | all-gather | bytes 491520 | tf_op jit(solution)/shard_map/all_gather | solution.py:20
  142.2 16.9 %all-gather.14 = bf16[8,4,2,4,3,512]{5,3,4,2,1,0:T(4,128)(2,1)S(1)} all-gather(bf16[4,4,2,4,3,512]{5,3,4,2,1,0:T(4,128)(2,1)S(1)} %bitcast.145), channel_id=16, replica_groups=mesh['node_0'=4,'node_1'=2,'node_2'=4,'node_3'=2,'local'=4] {'node_3'}, dimensions={0}, use_global_device_ids=true | all-gather | bytes 1179648 | tf_op jit(solution)/shard_map/all_gather | solution.py:20
  160.7 7.1 all-gather.28
  167.8 9.0 all-gather.16
  176.8 10.3 %all-gather.17 = bf16[16,2,3,512]{3,1,2,0:T(2,128)(2,1)S(1)} all-gather(bf16[4,2,3,512]{3,1,2,0:T(2,128)(2,1)S(1)} %copy.141), channel_id=19, replica_groups=mesh['node_0'=4,'node_1'=2,'node_2'=4,'node_3'=2,'local'=4] {'local'}, dimensions={0}, use_global_device_ids=true | all-gather | bytes 122880 | tf_op jit(solution)/shard_map/all_gather | solution.py:20
  187.2 8.9 all-gather.18
  196.1 12.4 %all-gather.19 = bf16[8,4,4,2,3,512]{5,2,4,3,1,0:T(4,128)(2,1)S(1)} all-gather(bf16[2,4,4,2,3,512]{5,2,4,3,1,0:T(4,128)(2,1)S(1)} %bitcast.147), channel_id=21, replica_groups=mesh['node_0'=4,'node_1'=2,'node_2'=4,'node_3'=2,'local'=4] {'node_2'}, dimensions={0}, use_global_device_ids=true | all-gather | bytes 983040 | tf_op jit(solution)/shard_map/all_gather | solution.py:20
  210.9 10.2 %all-gather.25 = bf16[4,3,512]{2,1,0:T(4,128)(2,1)S(1)} all-gather(bf16[1,3,512]{2,1,0:T(4,128)(2,1)S(1)} %get-tuple-element.21), channel_id=2, replica_groups=mesh['node_0'=4,'node_1'=2,'node_2'=4,'node_3'=2,'local'=4] {'local'}, dimensions={0}, use_global_device_ids=true | all-gather | bytes 15360 | tf_op jit(solution)/shard_map/all_gather | solution.py:20
  221.1 6.3 all-gather.1
  227.5 9.8 %all-gather.2 = bf16[8,4,3,512]{3,1,2,0:T(4,128)(2,1)S(1)} all-gather(bf16[2,4,3,512]{3,1,2,0:T(4,128)(2,1)S(1)} %copy.133), channel_id=4, replica_groups=mesh['node_0'=4,'node_1'=2,'node_2'=4,'node_3'=2,'local'=4] {'node_2'}, dimensions={0}, use_global_device_ids=true | all-gather | bytes 122880 | tf_op jit(solution)/shard_map/all_gather | solution.py:20
  237.3 9.2 all-gather.3
  246.5 10.8 %all-gather.4 = bf16[8,4,2,4,3,512]{5,3,4,2,1,0:T(4,128)(2,1)S(1)} all-gather(bf16[2,4,2,4,3,512]{5,3,4,2,1,0:T(4,128)(2,1)S(1)} %bitcast.148), channel_id=6, replica_groups=mesh['node_0'=4,'node_1'=2,'node_2'=4,'node_3'=2,'local'=4] {'node_0'}, dimensions={0}, use_global_device_ids=true | all-gather | bytes 983040 | tf_op jit(solution)/shard_map/all_gather | solution.py:20
  269.5 6.2 fusion.15
  278.4 53.9 %concatenate.24 = bf16[256,16,512]{2,1,0:T(8,128)(2,1)} concatenate(bf16[256,3,512]{2,1,0:T(4,128)(2,1)} %bitcast.121, bf16[256,3,512]{2,1,0:T(4,128)(2,1)S(1)} %bitcast.119, bf16[256,3,512]{2,1,0:T(4,128)(2,1)} %bitcast.133, bf16[256,3,512]{2,1,0:T(4,128)(2,1)} %bitcast.134, bf16[256,4,512]{2,1,0:T(4,128)(2,1)} %bitcast.123), dimensions={1} | concatenate | bytes 8388608 | tf_op jit(solution)/shard_map/concatenate | solution.py:42
  341.0 6.1 fusion.20
  347.1 12.9 %fusion.13 = f32[4,8,256,256]{2,3,1,0:T(8,128)} fusion(f32[4,256,256,8]{2,1,3,0:T(8,128)} %fusion.20, pred[256,256]{0,1:T(8,128)(4,1)} %fusion.24), kind=kOutput, calls=%fused_computation.18 | output fusion | flops 12599806 | bytes 16842752 | tf_op jit(solution)/shard_map/div | solution.py:93
  360.0 14.2 %fusion.17 = f32[256,4,128]{2,0,1:T(8,128)} fusion(bf16[256,4,8,128]{0,3,2,1:T(8,128)(2,1)} %bitcast.128, f32[4,8,256,256]{2,3,1,0:T(8,128)} %fusion.13, f32[4,256,256,8]{2,1,3,0:T(8,128)} %fusion.15), kind=kOutput, calls=%fused_computation.22 | convolution fusion | flops 547365120 | bytes 19398656 | tf_op jit(solution)/shard_map/kgts,tkgd->skd/dot_general | solution.py:99
  382.1 9.0 copy.183
  397.9 53.9 %concatenate.32 = bf16[64,4,16,512]{3,2,1,0:T(8,128)(2,1)} concatenate(bf16[64,4,3,512]{3,2,1,0:T(4,128)(2,1)} %bitcast.122, bf16[64,4,3,512]{3,2,1,0:T(4,128)(2,1)S(1)} %bitcast.120, bf16[64,4,3,512]{3,2,1,0:T(4,128)(2,1)} %copy.164, bf16[64,4,3,512]{3,2,1,0:T(4,128)(2,1)} %copy.165, bf16[64,4,4,512]{3,2,1,0:T(4,128)(2,1)} %bitcast.124), dimensions={2} | concatenate | bytes 8388608 | tf_op jit(solution)/shard_map/concatenate | solution.py:42
  454.1 362.0 %reduce-scatter.4.cloned.1.call-done = f32[64,512]{1,0:T(8,128)} async-done(((f32[4096,512]{1,0:T(8,128)}), f32[64,512]{1,0:T(8,128)}) %reduce-scatter.4.cloned.1.call-update) | async-done | bytes 131088 | tf_op jit(solution)/shard_map/reduce_scatter | solution.py:129
  819.4 83.8 %all-gather.33.cloned.1.call-done = bf16[4096,512]{1,0:T(8,128)(2,1)} async-done(((bf16[1024,512]{1,0:T(8,128)(2,1)}), bf16[4096,512]{1,0:T(8,128)(2,1)}) %all-gather.33.cloned.1.call-update) | async-done | bytes 4194320 | tf_op jit(solution)/shard_map/all_gather | solution.py:123
  (58 shorter events, 72.4 us)
Async XLA Ops:
  7.2 325.1 %copy-start = (bf16[256,4096]{1,0:T(8,128)(2,1)S(1)}, bf16[256,4096]{1,0:T(8,128)(2,1)}, u32[]{:S(2)}) copy-start(bf16[256,4096]{1,0:T(8,128)(2,1)} %param.6) | copy-start | bytes 6291460
  7.2 268.5 %all-gather.35.cloned.1.call-start = ((), (), s32[]{:S(2)}) async-start(), calls=%async_computation.3 | async-start | bytes 1572864 | tf_op jit(solution)/shard_map/all_gather | solution.py:20
  49.0 767.1 %reduce-scatter.4.cloned.1.call-start = ((), (), s32[]{:S(2)}) async-start(), calls=%async_computation.4 | async-start | bytes 8519680 | tf_op jit(solution)/shard_map/reduce_scatter | solution.py:129
  159.1 99.9 %copy-start.1 = (bf16[8,4,2,4,3,512]{5,3,4,2,1,0:T(4,128)(2,1)}, bf16[8,4,2,4,3,512]{5,3,4,2,1,0:T(4,128)(2,1)S(1)}, u32[]{:S(2)}) copy-start(bf16[8,4,2,4,3,512]{5,3,4,2,1,0:T(4,128)(2,1)S(1)} %all-gather.14) | copy-start | bytes 2359300
  159.1 99.9 %copy-start.3 = (s32[256]{0:T(256)S(1)}, s32[256]{0:T(256)}, u32[]{:S(2)}) copy-start(s32[256]{0:T(256)} %param.11) | copy-start | bytes 3076
  208.4 0.9 copy-start.2
  391.2 512.0 %all-gather.33.cloned.1.call-start = ((), (), s32[]{:S(2)}) async-start(), calls=%async_computation.2 | async-start | bytes 5242880 | tf_op jit(solution)/shard_map/all_gather | solution.py:123
  816.0 103.3 %all-to-all-start = ((f32[4,16,512]{2,1,0:T(8,128)}), f32[4,16,512]{2,1,0:T(8,128)S(1)}, u32[]{:S(2)}, u32[]{:S(2)}) async-start(f32[4,16,512]{2,1,0:T(8,128)} %bitcast.161), calls=%async_computation | async-start | bytes 262144 | tf_op jit(solution)/shard_map/all_to_all | solution.py:53
Sparse Core Ops, SparseCore 0:
  49.1 42.8 all-gather.34
  391.3 424.6 reduce-scatter.3
  818.4 84.6 all-gather.32
where the time goes:
time: 934 us; the launch traced here: 926 us
  waiting for transfers between devices  446 us (48%)
  blocking collectives  243 us (26%)
  local copies, waits for them, and re-layouts  162 us (17%)
  matrix products  39.3 us (4%)
  other arithmetic  19.2 us (2%)
  between operations  13.9 us (1%)
    reduce_scatter x1, waiting for transfers between devices, per_device(): lax.psum_scatter(lax.dot_general(tokens, grad_keys, (((0,), (0,)), ((), (...  362 us
    all_gather x24, blocking collectives, stacked_from(): tiles = lax.all_gather(tiles, axes[k])  243 us
    concatenate x4, local copies, waits for them, and re-layouts, gather_at_once(): return in_order(jnp.concatenate(outs, axis=widest + 1), dim)  111 us
    all_gather x1, waiting for transfers between devices, per_device(): lax.all_gather(quarter, 'local', axis=0, tiled=True)  83.8 us
    unnamed x15, local copies, waits for them, and re-layouts  22.1 us
  transfers between devices with their start and end apart: 4, of which 2 were waited for; matrix products, arithmetic and copies ran while one was open for 11% of the time, Pallas kernels for 0%

commit v1 on v0

--- a/solution.py
+++ b/solution.py
@@ -120,7 +120,15 @@
     grad_keys = rotate(grad_rot, cosine, sine_part, head_width, -1.0).astype(jnp.bfloat16)
     mixed = lax.dot_general(
         grad_keys,
-        lax.all_gather(quarter, "local", axis=0, tiled=True),
+        jnp.concatenate(
+            lax.all_to_all(
+                jnp.stack([quarter for _ in range(lax.axis_size("local"))], 0),
+                axis_name="local",
+                split_axis=0,
+                concat_axis=0,
+            ),
+            axis=0,
+        ),
         (((1,), (1,)), ((), ())),
         preferred_element_type=jnp.float32,
     ).astype(jnp.bfloat16)

time: 934 us -> 868 us (0.929)
  waiting for transfers between devices: 446 us -> 250 us
  blocking collectives: 243 us -> 361 us
    all_to_all x0 -> x1, blocking collectives: none -> 118 us  [per_device(): lax.all_to_all(jnp.stack([quarter for _ in range(lax.axis_size('local'))]...]
    reduce_scatter x1, waiting for transfers between devices: 362 us -> 250 us  [per_device(): lax.psum_scatter(lax.dot_general(tokens, grad_keys, (((0,), (0,)), ((), (...]
    all_gather x1 -> x0, waiting for transfers between devices: 83.8 us -> none  [per_device(): lax.all_gather(quarter, 'local', axis=0, tiled=True)]
  transfers between devices with their start and end apart: 4 -> 3, of which waited for: 2 -> 1; matrix products, arithmetic and copies ran while one was open for 11% -> 12% of each run, Pallas kernels for 0% -> 0%
where the time goes in v1:
time: 868 us; the launch traced here: 852 us
  blocking collectives  361 us (42%)
  waiting for transfers between devices  250 us (29%)
  local copies, waits for them, and re-layouts  161 us (19%)
  matrix products  39.3 us (5%)
  other arithmetic  19.2 us (2%)
  between operations  14.2 us (2%)
    reduce_scatter x1, waiting for transfers between devices, per_device(): lax.psum_scatter(lax.dot_general(tokens, grad_keys, (((0,), (0,)), ((), (...  250 us
    all_gather x24, blocking collectives, stacked_from(): tiles = lax.all_gather(tiles, axes[k])  243 us
    all_to_all x1, blocking collectives, per_device(): lax.all_to_all(jnp.stack([quarter for _ in range(lax.axis_size('local'))]...  118 us
    concatenate x4, local copies, waits for them, and re-layouts, gather_at_once(): return in_order(jnp.concatenate(outs, axis=widest + 1), dim)  111 us
    unnamed x15, local copies, waits for them, and re-layouts  22.1 us
  transfers between devices with their start and end apart: 3, of which 1 were waited for; matrix products, arithmetic and copies ran while one was open for 12% of the time, Pallas kernels for 0%

profile of v1, /device:TPU:1, one launch (start us, length us, event | category | flops | bytes accessed | tf_op | source)
XLA Modules:
  0.0 851.8 jit_solution(6088683768232004462)
XLA Ops:
  8.1 10.4 %all-gather.29 = bf16[4,4,512]{2,1,0:T(4,128)(2,1)S(1)} all-gather(bf16[1,4,512]{2,1,0:T(4,128)(2,1)S(1)} %slice_bitcast_fusion), channel_id=22, replica_groups=mesh['node_0'=4,'node_1'=2,'node_2'=4,'node_3'=2,'local'=4] {'node_0'}, dimensions={0}, use_global_device_ids=true | all-gather | bytes 20480 | tf_op jit(solution)/shard_map/all_gather | solution.py:20
  18.4 11.4 %all-gather.21 = bf16[16,4,512]{2,1,0:T(4,128)(2,1)S(1)} all-gather(bf16[4,4,512]{2,1,0:T(4,128)(2,1)S(1)} %all-gather.29), channel_id=23, replica_groups=mesh['node_0'=4,'node_1'=2,'node_2'=4,'node_3'=2,'local'=4] {'local'}, dimensions={0}, use_global_device_ids=true | all-gather | bytes 81920 | tf_op jit(solution)/shard_map/all_gather | solution.py:20
  29.9 8.1 all-gather.22
  38.0 10.9 %all-gather.23 = bf16[8,4,4,4,512]{4,3,2,1,0:T(4,128)(2,1)} all-gather(bf16[2,4,4,4,512]{4,3,2,1,0:T(4,128)(2,1)S(1)} %bitcast.152), channel_id=25, replica_groups=mesh['node_0'=4,'node_1'=2,'node_2'=4,'node_3'=2,'local'=4] {'node_2'}, dimensions={0}, use_global_device_ids=true | all-gather | bytes 655360 | tf_op jit(solution)/shard_map/all_gather | solution.py:20
  54.3 9.0 %all-gather.6 = bf16[8,3,512]{2,1,0:T(4,128)(2,1)S(1)} all-gather(bf16[2,3,512]{2,1,0:T(4,128)(2,1)S(1)} %all-gather.26), channel_id=8, replica_groups=mesh['node_0'=4,'node_1'=2,'node_2'=4,'node_3'=2,'local'=4] {'node_2'}, dimensions={0}, use_global_device_ids=true | all-gather | bytes 30720 | tf_op jit(solution)/shard_map/all_gather | solution.py:20
  63.3 7.9 all-gather.7
  71.3 10.6 %all-gather.8 = bf16[8,4,2,3,512]{4,1,3,2,0:T(4,128)(2,1)S(1)} all-gather(bf16[2,4,2,3,512]{4,1,3,2,0:T(4,128)(2,1)S(1)} %copy.136), channel_id=10, replica_groups=mesh['node_0'=4,'node_1'=2,'node_2'=4,'node_3'=2,'local'=4] {'node_0'}, dimensions={0}, use_global_device_ids=true | all-gather | bytes 245760 | tf_op jit(solution)/shard_map/all_gather | solution.py:20
  81.9 21.4 %all-gather.9 = bf16[16,2,4,2,3,512]{5,2,4,3,1,0:T(4,128)(2,1)S(1)} all-gather(bf16[4,2,4,2,3,512]{5,2,4,3,1,0:T(4,128)(2,1)S(1)} %bitcast.151), channel_id=11, replica_groups=mesh['node_0'=4,'node_1'=2,'node_2'=4,'node_3'=2,'local'=4] {'local'}, dimensions={0}, use_global_device_ids=true | all-gather | bytes 983040 | tf_op jit(solution)/shard_map/all_gather | solution.py:20
  104.6 9.6 %all-gather.27 = bf16[4,3,512]{2,1,0:T(4,128)(2,1)S(1)} all-gather(bf16[1,3,512]{2,1,0:T(4,128)(2,1)S(1)} %get-tuple-element.19), channel_id=12, replica_groups=mesh['node_0'=4,'node_1'=2,'node_2'=4,'node_3'=2,'local'=4] {'node_2'}, dimensions={0}, use_global_device_ids=true | all-gather | bytes 15360 | tf_op jit(solution)/shard_map/all_gather | solution.py:20
  114.2 7.2 all-gather.11
  121.4 9.3 %all-gather.12 = bf16[8,4,3,512]{3,1,2,0:T(4,128)(2,1)S(1)} all-gather(bf16[2,4,3,512]{3,1,2,0:T(4,128)(2,1)S(1)} %copy.139), channel_id=14, replica_groups=mesh['node_0'=4,'node_1'=2,'node_2'=4,'node_3'=2,'local'=4] {'node_0'}, dimensions={0}, use_global_device_ids=true | all-gather | bytes 122880 | tf_op jit(solution)/shard_map/all_gather | solution.py:20
  130.7 11.4 %all-gather.13 = bf16[16,2,4,3,512]{4,2,3,1,0:T(4,128)(2,1)S(1)} all-gather(bf16[4,2,4,3,512]{4,2,3,1,0:T(4,128)(2,1)S(1)} %bitcast.156), channel_id=15, replica_groups=mesh['node_0'=4,'node_1'=2,'node_2'=4,'node_3'=2,'local'=4] {'local'}, dimensions={0}, use_global_device_ids=true | all-gather | bytes 491520 | tf_op jit(solution)/shard_map/all_gather | solution.py:20
  142.2 16.9 %all-gather.14 = bf16[8,4,2,4,3,512]{5,3,4,2,1,0:T(4,128)(2,1)S(1)} all-gather(bf16[4,4,2,4,3,512]{5,3,4,2,1,0:T(4,128)(2,1)S(1)} %bitcast.147), channel_id=16, replica_groups=mesh['node_0'=4,'node_1'=2,'node_2'=4,'node_3'=2,'local'=4] {'node_3'}, dimensions={0}, use_global_device_ids=true | all-gather | bytes 1179648 | tf_op jit(solution)/shard_map/all_gather | solution.py:20
  160.7 7.1 all-gather.28
  167.8 9.0 %all-gather.16 = bf16[8,3,512]{2,1,0:T(4,128)(2,1)S(1)} all-gather(bf16[2,3,512]{2,1,0:T(4,128)(2,1)S(1)} %all-gather.28), channel_id=18, replica_groups=mesh['node_0'=4,'node_1'=2,'node_2'=4,'node_3'=2,'local'=4] {'node_0'}, dimensions={0}, use_global_device_ids=true | all-gather | bytes 30720 | tf_op jit(solution)/shard_map/all_gather | solution.py:20
  176.8 10.3 %all-gather.17 = bf16[16,2,3,512]{3,1,2,0:T(2,128)(2,1)S(1)} all-gather(bf16[4,2,3,512]{3,1,2,0:T(2,128)(2,1)S(1)} %copy.141), channel_id=19, replica_groups=mesh['node_0'=4,'node_1'=2,'node_2'=4,'node_3'=2,'local'=4] {'local'}, dimensions={0}, use_global_device_ids=true | all-gather | bytes 122880 | tf_op jit(solution)/shard_map/all_gather | solution.py:20
  187.2 8.9 %all-gather.18 = bf16[8,4,2,3,512]{4,1,3,2,0:T(4,128)(2,1)S(1)} all-gather(bf16[4,4,2,3,512]{4,1,3,2,0:T(4,128)(2,1)S(1)} %copy.142), channel_id=20, replica_groups=mesh['node_0'=4,'node_1'=2,'node_2'=4,'node_3'=2,'local'=4] {'node_3'}, dimensions={0}, use_global_device_ids=true | all-gather | bytes 294912 | tf_op jit(solution)/shard_map/all_gather | solution.py:20
  196.1 12.4 %all-gather.19 = bf16[8,4,4,2,3,512]{5,2,4,3,1,0:T(4,128)(2,1)S(1)} all-gather(bf16[2,4,4,2,3,512]{5,2,4,3,1,0:T(4,128)(2,1)S(1)} %bitcast.149), channel_id=21, replica_groups=mesh['node_0'=4,'node_1'=2,'node_2'=4,'node_3'=2,'local'=4] {'node_2'}, dimensions={0}, use_global_device_ids=true | all-gather | bytes 983040 | tf_op jit(solution)/shard_map/all_gather | solution.py:20
  210.9 10.2 %all-gather.25 = bf16[4,3,512]{2,1,0:T(4,128)(2,1)S(1)} all-gather(bf16[1,3,512]{2,1,0:T(4,128)(2,1)S(1)} %get-tuple-element.21), channel_id=2, replica_groups=mesh['node_0'=4,'node_1'=2,'node_2'=4,'node_3'=2,'local'=4] {'local'}, dimensions={0}, use_global_device_ids=true | all-gather | bytes 15360 | tf_op jit(solution)/shard_map/all_gather | solution.py:20
  221.1 6.3 all-gather.1
  227.5 9.8 %all-gather.2 = bf16[8,4,3,512]{3,1,2,0:T(4,128)(2,1)S(1)} all-gather(bf16[2,4,3,512]{3,1,2,0:T(4,128)(2,1)S(1)} %copy.133), channel_id=4, replica_groups=mesh['node_0'=4,'node_1'=2,'node_2'=4,'node_3'=2,'local'=4] {'node_2'}, dimensions={0}, use_global_device_ids=true | all-gather | bytes 122880 | tf_op jit(solution)/shard_map/all_gather | solution.py:20
  237.3 9.2 %all-gather.3 = bf16[8,2,4,3,512]{4,2,3,1,0:T(4,128)(2,1)S(1)} all-gather(bf16[4,2,4,3,512]{4,2,3,1,0:T(4,128)(2,1)S(1)} %bitcast.155), channel_id=5, replica_groups=mesh['node_0'=4,'node_1'=2,'node_2'=4,'node_3'=2,'local'=4] {'node_1'}, dimensions={0}, use_global_device_ids=true | all-gather | bytes 294912 | tf_op jit(solution)/shard_map/all_gather | solution.py:20
  246.5 10.8 %all-gather.4 = bf16[8,4,2,4,3,512]{5,3,4,2,1,0:T(4,128)(2,1)S(1)} all-gather(bf16[2,4,2,4,3,512]{5,3,4,2,1,0:T(4,128)(2,1)S(1)} %bitcast.150), channel_id=6, replica_groups=mesh['node_0'=4,'node_1'=2,'node_2'=4,'node_3'=2,'local'=4] {'node_0'}, dimensions={0}, use_global_device_ids=true | all-gather | bytes 983040 | tf_op jit(solution)/shard_map/all_gather | solution.py:20
  269.4 6.2 fusion.15
  278.4 53.8 %concatenate.23 = bf16[256,16,512]{2,1,0:T(8,128)(2,1)} concatenate(bf16[256,3,512]{2,1,0:T(4,128)(2,1)} %bitcast.123, bf16[256,3,512]{2,1,0:T(4,128)(2,1)S(1)} %bitcast.121, bf16[256,3,512]{2,1,0:T(4,128)(2,1)} %bitcast.135, bf16[256,3,512]{2,1,0:T(4,128)(2,1)} %bitcast.136, bf16[256,4,512]{2,1,0:T(4,128)(2,1)} %bitcast.125), dimensions={1} | concatenate | bytes 8388608 | tf_op jit(solution)/shard_map/concatenate | solution.py:42
  347.0 12.9 %fusion.13 = f32[4,8,256,256]{2,3,1,0:T(8,128)} fusion(f32[4,256,256,8]{2,1,3,0:T(8,128)} %fusion.20, pred[256,256]{0,1:T(8,128)(4,1)} %fusion.24), kind=kOutput, calls=%fused_computation.18 | output fusion | flops 12599806 | bytes 16842752 | tf_op jit(solution)/shard_map/div | solution.py:93
  359.9 14.2 %fusion.17 = f32[256,4,128]{2,0,1:T(8,128)} fusion(bf16[256,4,8,128]{0,3,2,1:T(8,128)(2,1)} %bitcast.130, f32[4,8,256,256]{2,3,1,0:T(8,128)} %fusion.13, f32[4,256,256,8]{2,1,3,0:T(8,128)} %fusion.15), kind=kOutput, calls=%fused_computation.22 | convolution fusion | flops 547365120 | bytes 19398656 | tf_op jit(solution)/shard_map/kgts,tkgd->skd/dot_general | solution.py:99
  382.1 9.0 %copy.183 = f32[4096,512]{1,0:T(8,128)} copy(f32[4096,512]{0,1:T(8,128)} %convolution_bitcast_fusion) | data formatting | bytes 16777216
  397.6 53.8 %concatenate.31 = bf16[64,4,16,512]{3,2,1,0:T(8,128)(2,1)} concatenate(bf16[64,4,3,512]{3,2,1,0:T(4,128)(2,1)} %bitcast.124, bf16[64,4,3,512]{3,2,1,0:T(4,128)(2,1)S(1)} %bitcast.122, bf16[64,4,3,512]{3,2,1,0:T(4,128)(2,1)} %copy.164, bf16[64,4,3,512]{3,2,1,0:T(4,128)(2,1)} %copy.165, bf16[64,4,4,512]{3,2,1,0:T(4,128)(2,1)} %bitcast.126), dimensions={2} | concatenate | bytes 8388608 | tf_op jit(solution)/shard_map/concatenate | solution.py:42
  453.1 118.3 %all_to_all.10 = bf16[4,1024,512]{2,1,0:T(8,128)(2,1)} all-to-all(bf16[4,1024,512]{2,1,0:T(8,128)(2,1)S(1)} %stack.3), channel_id=1, replica_groups=mesh['node_0'=4,'node_1'=2,'node_2'=4,'node_3'=2,'local'=4] {'local'}, dimensions={0} | all-to-all | bytes 8388608 | tf_op jit(solution)/shard_map/all_to_all | solution.py:124
  571.4 249.6 %reduce-scatter.4.cloned.1.call-done = f32[64,512]{1,0:T(8,128)} async-done(((f32[4096,512]{1,0:T(8,128)}), f32[64,512]{1,0:T(8,128)}) %reduce-scatter.4.cloned.1.call-update) | async-done | bytes 131088 | tf_op jit(solution)/shard_map/reduce_scatter | solution.py:137
  821.0 7.2 all-to-all-start.1
  (57 shorter events, 74.2 us)
Async XLA Ops:
  7.2 325.0 %copy-start = (bf16[256,4096]{1,0:T(8,128)(2,1)S(1)}, bf16[256,4096]{1,0:T(8,128)(2,1)}, u32[]{:S(2)}) copy-start(bf16[256,4096]{1,0:T(8,128)(2,1)} %param.6) | copy-start | bytes 6291460
  7.2 268.4 %all-gather.32.cloned.1.call-start = ((), (), s32[]{:S(2)}) async-start(), calls=%async_computation.3 | async-start | bytes 1572864 | tf_op jit(solution)/shard_map/all_gather | solution.py:20
  49.0 772.0 %reduce-scatter.4.cloned.1.call-start = ((), (), s32[]{:S(2)}) async-start(), calls=%async_computation.4 | async-start | bytes 8519680 | tf_op jit(solution)/shard_map/reduce_scatter | solution.py:137
  159.1 99.9 %copy-start.1 = (bf16[8,4,2,4,3,512]{5,3,4,2,1,0:T(4,128)(2,1)}, bf16[8,4,2,4,3,512]{5,3,4,2,1,0:T(4,128)(2,1)S(1)}, u32[]{:S(2)}) copy-start(bf16[8,4,2,4,3,512]{5,3,4,2,1,0:T(4,128)(2,1)S(1)} %all-gather.14) | copy-start | bytes 2359300
  159.1 99.9 %copy-start.3 = (s32[256]{0:T(256)S(1)}, s32[256]{0:T(256)}, u32[]{:S(2)}) copy-start(s32[256]{0:T(256)} %param.11) | copy-start | bytes 3076
  208.4 0.9 copy-start.2
  821.0 23.4 %all-to-all-start.1 = ((f32[4,16,512]{2,1,0:T(8,128)}), f32[4,16,512]{2,1,0:T(8,128)S(1)}, u32[]{:S(2)}, u32[]{:S(2)}) async-start(f32[4,16,512]{2,1,0:T(8,128)} %bitcast.163), calls=%async_computation.1 | async-start | bytes 262144 | tf_op jit(solution)/shard_map/all_to_all | solution.py:53
Sparse Core Ops, SparseCore 0:
  49.1 42.8 all-gather.31
  391.3 429.7 reduce-scatter.3
